TPU v7x, 256 devices: a whole 4x4x8 slice. The times are simulated.
256 devices in a mesh: section: 2 (over core), blk: 16 (over y_hi, z), head: 8 (over y_lo, x).
Axes of the slice: x: 4, y: 4 (y_hi: 2, y_lo: 2; y = y_hi * 2 + y_lo), z: 8, core: 2. Of those that a mesh axis runs over, the one named last changes fastest.
Arguments:
- projected: bfloat16 [16384, 8192], P(('section', 'blk')), may hold values from -6 to 6
- key_weight: bfloat16 [8192, 1024], P(None, 'head'), may hold values from -0.0625 to 0.0625
- value_weight: bfloat16 [8192, 1024], P(None, 'head'), may hold values from -0.0625 to 0.0625
- key_gain: float32 [128], replicated, may hold values from 0.1 to 1.9
- queries: bfloat16 [2048, 8, 1024], P('blk', 'section', 'head'), may hold values from -320 to 320
- frame_tokens: int32 [32], replicated, may hold values from 1 to 1024, 16384 in all
- span_first: int32 [2048], replicated, may hold values from 0 to 31
- span_count: int32 [2048], replicated, may hold values from 1 to 32
Outputs:
- attended: bfloat16 [2048, 8, 1024], P('blk', 'section', 'head')
Inputs may be any that keep to these rules, and one draw needn't show every extreme that they name: Frame f holds frame_tokens[f] consecutive visual tokens, and they sum to 16384.
All inputs are finite; a program needn't handle non-finite values.
Results may differ from a plain program's by a relative error of at most 0.005.
The roundings to bfloat16 on the way count: a program that leaves them out, or rounds other values in their place, can miss the bound.
Values may be sent and summed in bfloat16 or wider, within the bound.
A program may use at most 128 MiB of HBM per device.

v0:
```python
import jax
import jax.numpy as jnp
from jax import lax
from jax.sharding import PartitionSpec as P

HD = 128
FRAMES = 32


def span_bounds(frame_tokens, span_first, span_count):
    frame_ids = jnp.arange(FRAMES, dtype=jnp.int32)
    span_end = jnp.minimum(span_first + span_count, FRAMES)
    first_token = jnp.sum(
        jnp.where(frame_ids[None, :] < span_first[:, None], frame_tokens[None, :], 0), axis=1
    )
    end_token = jnp.sum(
        jnp.where(frame_ids[None, :] < span_end[:, None], frame_tokens[None, :], 0), axis=1
    )
    return (first_token, end_token)


def make_tables(projected, key_weight, value_weight, key_gain):
    count_rows = projected.shape[0]
    local_heads = key_weight.shape[1] // HD
    key_raw = jnp.dot(projected, key_weight, preferred_element_type=jnp.float32).reshape(
        count_rows, local_heads, HD
    )
    mean_square = jnp.mean(key_raw * key_raw, axis=2, keepdims=True)
    key_block = (key_raw / jnp.sqrt(mean_square + 1e-05) * key_gain).astype(jnp.bfloat16)
    value_block = (
        jnp.dot(projected, value_weight, preferred_element_type=jnp.float32)
        .astype(jnp.bfloat16)
        .reshape(count_rows, local_heads, HD)
    )
    return (key_block, value_block)


def masked_scores(query_block, key_block, key_positions, first_token, end_token):
    scores = jnp.einsum(
        "npgd,mgd->gnpm", query_block, key_block, preferred_element_type=jnp.float32
    ) * HD ** (-0.5)
    allowed = (key_positions[None, :] >= first_token[:, None]) & (
        key_positions[None, :] < end_token[:, None]
    )
    return jnp.where(allowed[None, :, None, :], scores, -1e30)


def weighted_sum(scores, row_max, value_block):
    weights = jnp.exp(scores - row_max[..., None])
    denominator = jnp.sum(weights, axis=3)
    numerator = jnp.einsum(
        "gnpm,mgd->npgd",
        weights.astype(jnp.bfloat16),
        value_block,
        preferred_element_type=jnp.float32,
    )
    return (numerator, jnp.transpose(denominator, (1, 2, 0)))


def body(
    projected, key_weight, value_weight, key_gain, queries, frame_tokens, span_first, span_count
):
    key_block, value_block = make_tables(projected, key_weight, value_weight, key_gain)
    first_token, end_token = span_bounds(frame_tokens, span_first, span_count)
    own_rows = queries.shape[0]
    sub_heads = queries.shape[1]
    local_heads = key_block.shape[1]
    count_rows = key_block.shape[0]
    section_count = lax.axis_size("section")
    block_count = lax.axis_size("blk")
    block_index = lax.axis_index("blk")
    section_ids = jnp.arange(section_count, dtype=jnp.int32)
    row_ids = jnp.arange(count_rows, dtype=jnp.int32)
    pair_keys, pair_values = (
        lax.all_gather(key_block, "section", axis=0, tiled=True),
        lax.all_gather(value_block, "section", axis=0, tiled=True),
    )
    all_keys, all_values = (
        lax.all_gather(pair_keys, "blk", axis=0, tiled=True),
        lax.all_gather(pair_values, "blk", axis=0, tiled=True),
    )
    block_ids = jnp.arange(block_count, dtype=jnp.int32)
    key_positions = (
        (section_ids[None, :, None] * block_count + block_ids[:, None, None]) * count_rows
        + row_ids[None, None, :]
    ).reshape(-1)
    own_first = lax.dynamic_slice_in_dim(first_token, block_index * own_rows, own_rows)
    own_end = lax.dynamic_slice_in_dim(end_token, block_index * own_rows, own_rows)
    shaped = queries.reshape(own_rows, sub_heads, local_heads, HD)
    scores = masked_scores(shaped, all_keys, key_positions, own_first, own_end)
    row_max = jnp.max(scores, axis=3)
    numerator, denominator = weighted_sum(scores, row_max, all_values)
    attended = numerator / denominator[..., None]
    return attended.astype(jnp.bfloat16).reshape(own_rows, sub_heads, local_heads * HD)


def solution(mesh):
    placed = (
        P(("section", "blk"), None),
        P(None, "head"),
        P(None, "head"),
        P(),
        P("blk", "section", "head"),
        P(),
        P(),
        P(),
    )
    return jax.shard_map(
        body, mesh=mesh, in_specs=placed, out_specs=P("blk", "section", "head"), check_vma=False
    )
```

profile of v0, /device:TPU:1, one launch (start us, length us, event | category | flops | bytes accessed | tf_op | source)
XLA Modules:
  0.0 239.1 jit_solution(14309865741915471274)
XLA Ops:
  6.5 0.0 copy-start
  6.5 0.0 copy-start.3
  6.5 0.0 all-gather.9.cloned.1.call-start
  6.5 1.6 copy-done
  8.1 6.3 %multiply_reduce_fusion = (f32[512]{0:T(512)S(1)}, f32[512,128]{0,1:T(8,128)S(1)}) fusion(bf16[512,8192]{1,0:T(8,128)(2,1)} %param.8, bf16[8192,128]{1,0:T(8,128)(2,1)S(1)} %copy-done), kind=kOutput, calls=%fused_computation.15 | convolution fusion | flops 1073872384 | bytes 10749952 | tf_op jit(solution)/shard_map/dot_general | solution.py:25
  14.4 0.0 copy-start.1
  14.4 0.0 copy-start.2
  14.4 0.0 copy-start.4
  14.4 0.0 copy-start.5
  14.5 0.0 copy-done.3
  14.5 0.1 multiply_convert_fusion
  14.6 5.0 %all-gather.2 = bf16[1024,128]{0,1:T(8,128)(2,1)} all-gather(bf16[512,128]{0,1:T(8,128)(2,1)S(1)} %multiply_convert_fusion), channel_id=4, replica_groups=mesh['section'=2,'blk'=16,'head'=8] {'section'}, dimensions={0}, use_global_device_ids=true | all-gather | bytes 393216 | tf_op jit(solution)/shard_map/all_gather | solution.py:75
  19.6 0.0 all-gather.9.cloned.1.call-update
  19.6 0.0 all-gather.7.cloned.1.call-start
  19.6 6.9 %convolution_convert_fusion = bf16[512,128]{0,1:T(8,128)(2,1)S(1)} fusion(bf16[512,8192]{1,0:T(8,128)(2,1)} %param.8, bf16[8192,128]{1,0:T(8,128)(2,1)} %param.10), kind=kOutput, calls=%fused_computation.12 | convolution fusion | flops 1073807360 | bytes 10616832 | tf_op jit(solution)/shard_map/dot_general | solution.py:31
  26.5 2.3 all-gather
  28.8 0.0 all-gather.7.cloned.1.call-update
  28.9 0.0 copy-done.1
  28.9 0.0 copy-done.2
  28.9 0.0 copy-done.4
  28.9 0.2 select_reduce_fusion.1
  29.1 0.1 dynamic_slice.6
  29.1 0.1 dynamic_slice.7
  29.2 0.1 add_bitcast_fusion
  29.3 8.3 %compare_and_fusion = pred[128,16384]{0,1:T(8,128)(4,1)} fusion(s32[128]{0:T(128)S(1)} %dynamic_slice.7, s32[128]{0:T(128)S(1)} %dynamic_slice.6, s32[16384]{0:T(1024)S(1)} %bitcast.37), kind=kLoop, calls=%fused_computation.6 | loop fusion | flops 6291456 | bytes 2163712 | tf_op jit(solution)/shard_map/and | solution.py:42
  37.6 79.9 %all-gather.9.cloned.1.call-done = bf16[16384,128]{0,1:T(8,128)(2,1)} async-done(((bf16[1024,128]{0,1:T(8,128)(2,1)}), bf16[16384,128]{0,1:T(8,128)(2,1)}) %all-gather.9.cloned.1.call-update) | async-done | bytes 4194320 | tf_op jit(solution)/shard_map/all_gather | solution.py:79
  117.5 0.0 copy-done.5
  117.5 17.4 %fusion.28 = (f32[128,4]{0,1:T(4,128)S(1)}, f32[128,4,16384]{0,2,1:T(8,128)}) fusion(bf16[128,4,128]{2,1,0:T(4,128)(2,1)S(1)} %copy-done.5, bf16[16384,128]{0,1:T(8,128)(2,1)} %all-gather.9.cloned.1.call-done, pred[128,16384]{0,1:T(8,128)(4,1)} %compare_and_fusion), kind=kOutput, calls=%fused_computation.26 | convolution fusion | flops 2172648960 | bytes 39979008 | tf_op jit(solution)/shard_map/npgd,mgd->gnpm/dot_general | solution.py:39
  134.9 15.1 %fusion = f32[128,4]{0,1:T(4,128)S(1)} fusion(f32[128,4,16384]{0,2,1:T(8,128)} %get-tuple-element.10, f32[128,4]{0,1:T(4,128)S(1)} %get-tuple-element.9), kind=kLoop, calls=%fused_computation.2 | loop fusion | flops 16776704 | bytes 33558528 | tf_op jit(solution)/shard_map/reduce_sum | solution.py:50
  150.0 66.7 %all-gather.7.cloned.1.call-done = bf16[16384,128]{0,1:T(8,128)(2,1)} async-done(((bf16[1024,128]{0,1:T(8,128)(2,1)}), bf16[16384,128]{0,1:T(8,128)(2,1)}) %all-gather.7.cloned.1.call-update) | async-done | bytes 4194320 | tf_op jit(solution)/shard_map/all_gather | solution.py:80
  216.7 14.7 %fusion.22 = bf16[128,4,128]{0,2,1:T(8,128)(2,1)S(1)} fusion(f32[128,4,16384]{0,2,1:T(8,128)} %get-tuple-element.10, f32[128,4]{0,1:T(4,128)S(1)} %get-tuple-element.9, bf16[16384,128]{0,1:T(8,128)(2,1)} %all-gather.7.cloned.1.call-done, f32[128,4]{0,1:T(4,128)S(1)} %fusion), kind=kOutput, calls=%fused_computation.13 | convolution fusion | flops 2164391936 | bytes 37883904 | tf_op jit(solution)/shard_map/gnpm,mgd->npgd/dot_general | solution.py:51
  231.4 0.8 copy.16
  (5 shorter events, 0.0 us)
Async XLA Ops:
  6.5 1.6 copy-start
  6.5 7.9 %copy-start.3 = (f32[128]{0:T(128)S(1)}, f32[128]{0:T(128)}, u32[]{:S(2)}) copy-start(f32[128]{0:T(128)} %param.11) | copy-start | bytes 1540
  6.5 111.0 %all-gather.9.cloned.1.call-start = ((), (), s32[]{:S(2)}) async-start(), calls=%async_computation.1 | async-start | bytes 4456448 | tf_op jit(solution)/shard_map/all_gather | solution.py:79
  14.4 14.4 %copy-start.1 = (s32[2048]{0:T(1024)S(1)}, s32[2048]{0:T(1024)}, u32[]{:S(2)}) copy-start(s32[2048]{0:T(1024)} %param.14) | copy-start | bytes 24580
  14.4 14.4 %copy-start.2 = (s32[2048]{0:T(1024)S(1)}, s32[2048]{0:T(1024)}, u32[]{:S(2)}) copy-start(s32[2048]{0:T(1024)} %param.15) | copy-start | bytes 24580
  14.4 14.5 %copy-start.4 = (s32[32]{0:T(128)S(1)}, s32[32]{0:T(128)}, u32[]{:S(2)}) copy-start(s32[32]{0:T(128)} %param.13) | copy-start | bytes 388
  14.4 103.1 %copy-start.5 = (bf16[128,4,128]{2,1,0:T(4,128)(2,1)S(1)}, bf16[128,4,128]{2,1,0:T(4,128)(2,1)}, u32[]{:S(2)}) copy-start(bf16[128,4,128]{2,1,0:T(4,128)(2,1)} %param.12) | copy-start | bytes 393220
  19.6 197.1 %all-gather.7.cloned.1.call-start = ((), (), s32[]{:S(2)}) async-start(), calls=%async_computation | async-start | bytes 4456448 | tf_op jit(solution)/shard_map/all_gather | solution.py:80
Sparse Core Ops, SparseCore 0:
  19.7 97.7 all-gather.8
  120.1 96.5 all-gather.6
where the time goes:
time: 242 us; the launch traced here: 239 us
  waiting for transfers between devices  147 us (61%)
  matrix products  45.2 us (19%)
  other arithmetic  23.8 us (10%)
  between operations  13.5 us (6%)
  blocking collectives  7.31 us (3%)
  local copies, waits for them, and re-layouts  2.58 us (1%)
    all_gather x1, waiting for transfers between devices, body(): lax.all_gather(pair_keys, 'blk', axis=0, tiled=True)  79.9 us
    all_gather x1, waiting for transfers between devices, body(): lax.all_gather(pair_values, 'blk', axis=0, tiled=True)  66.7 us
    dot_general x1, matrix products, masked_scores(): jnp.einsum('npgd,mgd->gnpm', query_block, key_block, preferred_element_ty...  17.4 us
    reduce_sum x1, other arithmetic, weighted_sum(): denominator = jnp.sum(weights, axis=3)  15.1 us
    dot_general x1, matrix products, weighted_sum(): jnp.einsum('gnpm,mgd->npgd', weights.astype(jnp.bfloat16), value_block, p...  14.7 us
    and x1, other arithmetic, masked_scores(): (key_positions[None, :] >= first_token[:, None]) & (key_positions[None, :...  8.29 us
    dot_general x1, matrix products, make_tables(): jnp.dot(projected, value_weight, preferred_element_type=jnp.float32)  6.86 us
    dot_general x1, matrix products, make_tables(): jnp.dot(projected, key_weight, preferred_element_type=jnp.float32)  6.27 us
  transfers between devices with their start and end apart: 2, of which 2 were waited for; matrix products, arithmetic and copies ran while one was open for 20% of the time, Pallas kernels for 0%

commit v1 on v0

v1 whole, which is shorter than its diff:
```python
import functools
import math

import jax
import jax.numpy as jnp
from jax import lax
from jax.experimental import pallas as pl
from jax.experimental.pallas import tpu as pltpu
from jax.sharding import PartitionSpec as P

HD = 128
FRAMES = 32
Z = 8
NEG = -1e30
SCALE = math.log2(math.e) / math.sqrt(HD)
EPS = 1e-05
ROW_TILE = 256
DEPTH = 1024
MESH = pl.DeviceIdType.MESH
f32 = jnp.float32
bf16 = jnp.bfloat16


def nt_dot(a, b):
    return lax.dot_general(a, b, (((1,), (1,)), ((), ())), preferred_element_type=f32)


def kernel(
    x_hbm, kw_hbm, vw_hbm, gain_ref, q_hbm, frames_ref, first_ref, count_ref,
    out_ref,
    xb, wb, raw, kv, kvs, qb, feat, ka, va, m_ref, acc_ref, o_send, o_recv, l_send, l_recv,
    in_sem, q_sem, r_send, r_recv, s_send, s_recv, qx_sem, ox_sem,
):
    steps = xb.shape[0]
    rows = qb.shape[1]
    part = kv.shape[2]
    sec = lax.axis_index("section")
    blk = lax.axis_index("blk")
    head = lax.axis_index("head")
    y_hi = blk // Z
    z = lax.rem(blk, Z)
    partner_blk = (1 - y_hi) * Z + z
    right = (sec, y_hi * Z + lax.rem(z + 1, Z), head)
    left = (sec, y_hi * Z + lax.rem(z + Z - 1, Z), head)
    partner = (sec, partner_blk, head)
    sibling = (1 - sec, blk, head)

    def in_copies(i):
        at = pl.ds(i * DEPTH, DEPTH)
        return (
            pltpu.make_async_copy(kw_hbm.at[at, :], wb.at[i, :, pl.ds(0, HD)], in_sem.at[0, i]),
            pltpu.make_async_copy(vw_hbm.at[at, :], wb.at[i, :, pl.ds(HD, HD)], in_sem.at[1, i]),
            pltpu.make_async_copy(x_hbm.at[:, at], xb.at[i], in_sem.at[2, i]),
        )

    own_q = pltpu.make_async_copy(q_hbm, qb.at[1], q_sem.at[0])
    own_q.start()
    for i in range(steps):
        for copy in in_copies(i):
            copy.start()

    barrier = pltpu.get_barrier_semaphore()
    for other in (right, left, partner, sibling):
        pl.semaphore_signal(barrier, inc=1, device_id=other, device_id_type=MESH)
    pl.semaphore_wait(barrier, 4)

    own_q.wait()
    q_copy = pltpu.make_async_remote_copy(
        src_ref=qb.at[1], dst_ref=qb.at[0], send_sem=qx_sem.at[0], recv_sem=qx_sem.at[1],
        device_id=partner, device_id_type=MESH,
    )
    q_copy.start()

    lane = lax.broadcasted_iota(jnp.int32, (1, HD), 1)
    starts = jnp.zeros((1, HD), jnp.int32)
    ends = jnp.zeros((1, HD), jnp.int32)
    for f in range(FRAMES):
        tokens = frames_ref[f]
        starts = starts + jnp.where(lane > f, tokens, 0)
        ends = ends + jnp.where(lane >= f, tokens, 0)
    ends = jnp.where(lane < FRAMES, ends, 0)
    heads_per_row = rows // first_ref.shape[1]
    text = first_ref.shape[1]
    spread = (
        lax.broadcasted_iota(jnp.int32, (rows, text), 0) // heads_per_row
        == lax.broadcasted_iota(jnp.int32, (rows, text), 1)
    ).astype(bf16)
    frame_id = lax.broadcasted_iota(jnp.int32, (HD, text), 0)
    for i, b in ((0, partner_blk), (1, blk)):
        first = first_ref[pl.ds(b, 1), :]
        end = jnp.minimum(first + count_ref[pl.ds(b, 1), :], FRAMES)
        closed = jnp.where((frame_id >= first) & (frame_id < end), 0.0, NEG).astype(bf16)
        feat[i] = nt_dot(spread, closed).astype(bf16)

    m_ref[...] = jnp.full_like(m_ref, 2 * NEG)
    acc_ref[...] = jnp.zeros_like(acc_ref)
    va[:, HD:] = jnp.ones_like(va[:, HD:])

    raw[...] = jnp.zeros_like(raw)

    def project(i, carry):
        for copy in in_copies(i):
            copy.wait()
        raw[...] += jnp.dot(xb[i], wb[i], preferred_element_type=f32)
        return carry

    lax.fori_loop(0, steps, project, 0)
    key_raw = raw[:, :HD]
    mean_square = jnp.mean(key_raw * key_raw, axis=1, keepdims=True)
    keys = (key_raw / jnp.sqrt(mean_square + EPS) * gain_ref[...]).astype(bf16)
    values = raw[:, HD:].astype(bf16)
    for j in range(2):
        kv[0, j, :, :HD] = keys[j * part : (j + 1) * part]
        kv[0, j, :, HD:] = values[j * part : (j + 1) * part]

    def ring_copy(direction, k, source):
        return pltpu.make_async_remote_copy(
            src_ref=source, dst_ref=kv.at[k + 1, direction],
            send_sem=r_send.at[direction, k], recv_sem=r_recv.at[direction, k],
            device_id=(right, left)[direction], device_id_type=MESH,
        )

    def to_sibling(e):
        return pltpu.make_async_remote_copy(
            src_ref=kv.at[e], dst_ref=kvs.at[e], send_sem=s_send.at[e], recv_sem=s_recv.at[e],
            device_id=sibling, device_id_type=MESH,
        )

    for k in range(2):
        ring_copy(0, k, kv.at[0, k]).start()
        ring_copy(1, k, kv.at[0, 1 - k]).start()
    to_sibling(0).start()

    def token_base(e, direction, section):
        hop = (e + 1) // 2
        if direction == 0:
            source, half = lax.rem(z + Z - hop, Z), lax.rem(e + 1, 2)
        else:
            source, half = lax.rem(z + hop, Z), lax.rem(e, 2)
        return ((section * 2 + y_hi) * Z + source) * (2 * part) + half * part

    def own_base(half, section):
        return ((section * 2 + y_hi) * Z + z) * (2 * part) + half * part

    def stage(slot, chunk, base):
        at = pl.ds(slot * part, part)
        pos = base + lax.broadcasted_iota(jnp.int32, (part, HD), 0)
        ka[at, :HD] = chunk[:, :HD]
        ka[at, HD:] = ((pos >= starts) & (pos < ends)).astype(bf16)
        va[at, :HD] = chunk[:, HD:]

    def attend(i, r, count):
        at = pl.ds(r * ROW_TILE, ROW_TILE)
        q = jnp.concatenate([qb[i, at, :], feat[i, at, :]], axis=1)
        k_all = ka[: count * part]
        v_all = va[: count * part]
        s = nt_dot(q, k_all)
        m_old = m_ref[i, at, :]
        m_new = jnp.maximum(m_old, jnp.max(s, axis=1, keepdims=True))
        p = jnp.exp2((s - m_new[:, :1]) * SCALE).astype(bf16)
        fade = jnp.exp2((m_old - m_new) * SCALE)
        m_ref[i, at, :] = m_new
        pv = jnp.dot(p, v_all, preferred_element_type=f32)
        acc_ref[i, at, :] = acc_ref[i, at, :] * jnp.concatenate([fade, fade], axis=1) + pv

    tiles = rows // ROW_TILE
    for j in range(2):
        stage(j, kv[0, j], own_base(j, sec))
    for r in range(tiles):
        attend(1, r, 2)
    q_copy.wait()
    for r in range(tiles):
        attend(0, r, 2)

    def arrivals(e, forward):
        for direction in range(2):
            ring_copy(direction, e - 1, kv.at[e, direction]).wait_recv()
            if forward:
                ring_copy(direction, e + 1, kv.at[e, direction]).start()
        to_sibling(e).start()
        to_sibling(e - 1).wait_recv()
        for direction in range(2):
            stage(direction, kv[e, direction], token_base(e, direction, sec))

    to_attend = [(i, r) for i in range(2) for r in range(tiles)]

    arrivals(1, True)
    for j in range(2):
        stage(2 + j, kvs[0, j], own_base(j, 1 - sec))
    for i, r in to_attend:
        attend(i, r, 4)

    def body(e, forward):
        arrivals(e, forward)
        for direction in range(2):
            stage(2 + direction, kvs[e - 1, direction], token_base(e - 1, direction, 1 - sec))
        for i, r in to_attend:
            attend(i, r, 4)

    def forwarding(e, carry):
        body(e, True)
        return carry

    def ending(e, carry):
        body(e, False)
        return carry

    lax.fori_loop(2, 6, forwarding, 0)
    lax.fori_loop(6, 8, ending, 0)

    to_sibling(7).wait_recv()
    for direction in range(2):
        stage(direction, kvs[7, direction], token_base(7, direction, 1 - sec))

    def o_copies(r):
        at = pl.ds(r * ROW_TILE, ROW_TILE)
        return (
            pltpu.make_async_remote_copy(
                src_ref=o_send.at[at, :], dst_ref=o_recv.at[at, :],
                send_sem=ox_sem.at[0, r], recv_sem=ox_sem.at[1, r],
                device_id=partner, device_id_type=MESH,
            ),
            pltpu.make_async_remote_copy(
                src_ref=l_send.at[r], dst_ref=l_recv.at[r],
                send_sem=ox_sem.at[2, r], recv_sem=ox_sem.at[3, r],
                device_id=partner, device_id_type=MESH,
            ),
        )

    def level(i, at):
        return m_ref[i, at, :] * SCALE + jnp.log2(acc_ref[i, at, HD:])

    for r in range(tiles):
        at = pl.ds(r * ROW_TILE, ROW_TILE)
        attend(0, r, 2)
        o_send[at, :] = (acc_ref[0, at, :HD] / acc_ref[0, at, HD:]).astype(bf16)
        weight = level(0, at)
        for h in range(ROW_TILE // HD):
            l_send[r, pl.ds(8 * h, 8), :] = weight[h * HD : (h + 1) * HD].T[:8]
        for copy in o_copies(r):
            copy.start()
    for r in range(tiles):
        attend(1, r, 2)
    for r in range(tiles):
        at = pl.ds(r * ROW_TILE, ROW_TILE)
        for copy in o_copies(r):
            copy.wait_recv()
        mine = level(1, at)
        theirs = jnp.concatenate(
            [
                jnp.broadcast_to(l_recv[r, 8 * h : 8 * h + 1, :], (HD, HD)).T
                for h in range(ROW_TILE // HD)
            ],
            axis=0,
        )
        top = jnp.maximum(mine, theirs)
        mine = jnp.exp2(mine - top)
        theirs = jnp.exp2(theirs - top)
        own = acc_ref[1, at, :HD] / acc_ref[1, at, HD:]
        total = (mine * own + theirs * o_recv[at, :].astype(f32)) / (mine + theirs)
        out_ref[at, :] = total.astype(bf16)

    for k in range(7):
        for direction in range(2):
            ring_copy(direction, k, kv.at[0, 0]).wait_send()
    for e in range(8):
        to_sibling(e).wait_send()
    for r in range(tiles):
        for copy in o_copies(r):
            copy.wait_send()


def body(
    projected, key_weight, value_weight, key_gain, queries, frame_tokens, span_first, span_count
):
    count, width = projected.shape
    text, sub_heads, _ = queries.shape
    rows = text * sub_heads
    part = count // 2
    steps = width // DEPTH
    anywhere = pl.BlockSpec(memory_space=pl.ANY)
    vmem = pl.BlockSpec(memory_space=pltpu.VMEM)
    out = pl.pallas_call(
        kernel,
        out_shape=jax.ShapeDtypeStruct((rows, HD), bf16),
        in_specs=[
            anywhere, anywhere, anywhere, vmem, anywhere,
            pl.BlockSpec(memory_space=pltpu.SMEM), vmem, vmem,
        ],
        out_specs=vmem,
        scratch_shapes=[
            pltpu.VMEM((steps, count, DEPTH), bf16),
            pltpu.VMEM((steps, DEPTH, 2 * HD), bf16),
            pltpu.VMEM((count, 2 * HD), f32),
            pltpu.VMEM((8, 2, part, 2 * HD), bf16),
            pltpu.VMEM((8, 2, part, 2 * HD), bf16),
            pltpu.VMEM((2, rows, HD), bf16),
            pltpu.VMEM((2, rows, HD), bf16),
            pltpu.VMEM((4 * part, 2 * HD), bf16),
            pltpu.VMEM((4 * part, 2 * HD), bf16),
            pltpu.VMEM((2, rows, HD), f32),
            pltpu.VMEM((2, rows, 2 * HD), f32),
            pltpu.VMEM((rows, HD), bf16),
            pltpu.VMEM((rows, HD), bf16),
            pltpu.VMEM((rows // ROW_TILE, 8 * (ROW_TILE // HD), HD), f32),
            pltpu.VMEM((rows // ROW_TILE, 8 * (ROW_TILE // HD), HD), f32),
            pltpu.SemaphoreType.DMA((3, steps)),
            pltpu.SemaphoreType.DMA((1,)),
            pltpu.SemaphoreType.DMA((2, 7)),
            pltpu.SemaphoreType.DMA((2, 7)),
            pltpu.SemaphoreType.DMA((8,)),
            pltpu.SemaphoreType.DMA((8,)),
            pltpu.SemaphoreType.DMA((2,)),
            pltpu.SemaphoreType.DMA((4, rows // ROW_TILE)),
        ],
        compiler_params=pltpu.CompilerParams(
            collective_id=0, has_side_effects=True, vmem_limit_bytes=50 * 2**20
        ),
        name="gather_attend",
    )(
        projected, key_weight, value_weight, key_gain.reshape(1, HD),
        queries.reshape(rows, HD), frame_tokens,
        span_first.reshape(-1, text), span_count.reshape(-1, text),
    )
    return out.reshape(text, sub_heads, HD)


def solution(mesh):
    placed = (
        P(("section", "blk"), None),
        P(None, "head"),
        P(None, "head"),
        P(),
        P("blk", "section", "head"),
        P(),
        P(),
        P(),
    )
    return jax.shard_map(
        body, mesh=mesh, in_specs=placed, out_specs=P("blk", "section", "head"), check_vma=False
    )
```

time: 242 us -> 48.7 us (0.20); the launches traced: 239 us -> 48.4 us
  waiting for transfers between devices: 147 us -> 0 us
  matrix products: 45.2 us -> 0 us
  Pallas kernels: 0 us -> 42.5 us
  other arithmetic: 23.8 us -> 0 us
  between operations: 13.5 us -> 0.02 us
  blocking collectives: 7.31 us -> 0 us
  local copies, waits for them, and re-layouts: 2.58 us -> 5.85 us
    all_gather x2 -> x0, waiting for transfers between devices: 147 us -> none  [the longest x1 79.9 us: body(): lax.all_gather(pair_keys, 'blk', axis=0, tiled=True)]
    dot_general x4 -> x0, matrix products: 45.2 us -> none  [the longest x1 17.4 us: masked_scores(): jnp.einsum('npgd,mgd->gnpm', query_block, key_block, preferred_element_ty...]
    pallas_call x0 -> x1, Pallas kernels: none -> 42.5 us  [body(): pl.pallas_call(kernel, out_shape=jax.ShapeDtypeStruct((rows, HD), bf16),...]
    reduce_sum x2 -> x0, other arithmetic: 15.3 us -> none  [the longest x1 15.1 us: weighted_sum(): denominator = jnp.sum(weights, axis=3)]
    and x1 -> x0, other arithmetic: 8.29 us -> none  [masked_scores(): (key_positions[None, :] >= first_token[:, None]) & (key_positions[None, :...]
    all_gather x2 -> x0, blocking collectives: 7.31 us -> none  [the longest x1 5 us: body(): lax.all_gather(key_block, 'section', axis=0, tiled=True)]
    unnamed x13, local copies, waits for them, and re-layouts: 1.63 us -> 5.85 us
  transfers between devices with their start and end apart: 2 -> 0, of which waited for: 2 -> 0; matrix products, arithmetic and copies ran while one was open for 20% -> 0% of each run, Pallas kernels for 0% -> 0%
where the time goes in v1:
time: 48.7 us; the launch traced here: 48.4 us
  Pallas kernels  42.5 us (87%)
  local copies, waits for them, and re-layouts  5.85 us (12%)
    pallas_call x1, Pallas kernels, body(): pl.pallas_call(kernel, out_shape=jax.ShapeDtypeStruct((rows, HD), bf16),...  42.5 us
    unnamed x13, local copies, waits for them, and re-layouts  5.85 us

profile of v1, /device:TPU:1, one launch (start us, length us, event | category | flops | bytes accessed | tf_op | source)
XLA Modules:
  0.0 48.4 jit_solution(14550788710706250337)
XLA Ops:
  0.0 0.0 copy-start
  0.0 1.6 %copy-done = bf16[8192,128]{1,0:T(8,128)(2,1)S(1)} copy-done((bf16[8192,128]{1,0:T(8,128)(2,1)S(1)}, bf16[8192,128]{1,0:T(8,128)(2,1)}, u32[]{:S(2)}) %copy-start) | copy-done | bytes 2097176
  1.6 0.0 copy-start.1
  1.6 0.9 %copy-done.1 = bf16[128,4,128]{2,1,0:T(4,128)(2,1)S(1)} copy-done((bf16[128,4,128]{2,1,0:T(4,128)(2,1)S(1)}, bf16[128,4,128]{2,1,0:T(4,128)(2,1)}, u32[]{:S(2)}) %copy-start.1) | copy-done | bytes 131096
  2.5 0.0 copy-start.2
  2.5 0.7 %copy-done.2 = s32[2048]{0:T(1024)S(1)} copy-done((s32[2048]{0:T(1024)S(1)}, s32[2048]{0:T(1024)}, u32[]{:S(2)}) %copy-start.2) | copy-done | bytes 8216
  3.2 0.0 copy-start.3
  3.2 0.7 %copy-done.3 = s32[2048]{0:T(1024)S(1)} copy-done((s32[2048]{0:T(1024)S(1)}, s32[2048]{0:T(1024)}, u32[]{:S(2)}) %copy-start.3) | copy-done | bytes 8216
  3.9 0.0 copy-start.4
  3.9 0.7 %copy-done.4 = f32[128]{0:T(128)S(1)} copy-done((f32[128]{0:T(128)S(1)}, f32[128]{0:T(128)}, u32[]{:S(2)}) %copy-start.4) | copy-done | bytes 536
  4.5 0.0 copy-start.5
  4.5 0.7 %copy-done.5 = s32[32]{0:T(128)S(1)} copy-done((s32[32]{0:T(128)S(1)}, s32[32]{0:T(128)}, u32[]{:S(2)}) %copy-start.5) | copy-done | bytes 152
  5.2 42.5 %gather_attend.1 = bf16[512,128]{1,0:T(8,128)(2,1)S(1)} custom-call(bf16[512,8192]{1,0:T(8,128)(2,1)} %x_hbm.1, bf16[8192,128]{1,0:T(8,128)(2,1)S(1)} %copy-done, bf16[8192,128]{1,0:T(8,128)(2,1)} %vw_hbm.1, f32[1,128]{1,0:T(1,128)S(1)} %bitcast.9, bf16[512,128]{1,0:T(8,128)(2,1)S(1)} %bitcast.6, s32[32]{0:T(128)S(1)} %copy-done.5, s32[16,128]{1,0:T(8,128)S(1)} %bitcast.7, ...), custom_call_target="tpu_custom_call" | custom-call | tf_op jit(solution)/shard_map/gather_attend/pallas_call | solution.py:283
  47.7 0.7 %copy.10 = bf16[128,4,128]{2,1,0:T(4,128)(2,1)} copy(bf16[128,4,128]{2,1,0:T(4,128)(2,1)S(1)} %bitcast.5) | data formatting | bytes 262144
Async XLA Ops:
  0.0 1.6 %copy-start = (bf16[8192,128]{1,0:T(8,128)(2,1)S(1)}, bf16[8192,128]{1,0:T(8,128)(2,1)}, u32[]{:S(2)}) copy-start(bf16[8192,128]{1,0:T(8,128)(2,1)} %kw_hbm.1) | copy-start | bytes 6291460
  1.6 0.9 %copy-start.1 = (bf16[128,4,128]{2,1,0:T(4,128)(2,1)S(1)}, bf16[128,4,128]{2,1,0:T(4,128)(2,1)}, u32[]{:S(2)}) copy-start(bf16[128,4,128]{2,1,0:T(4,128)(2,1)} %param.12) | copy-start | bytes 393220
  2.5 0.7 %copy-start.2 = (s32[2048]{0:T(1024)S(1)}, s32[2048]{0:T(1024)}, u32[]{:S(2)}) copy-start(s32[2048]{0:T(1024)} %param.14) | copy-start | bytes 24580
  3.2 0.7 %copy-start.3 = (s32[2048]{0:T(1024)S(1)}, s32[2048]{0:T(1024)}, u32[]{:S(2)}) copy-start(s32[2048]{0:T(1024)} %param.15) | copy-start | bytes 24580
  3.9 0.7 %copy-start.4 = (f32[128]{0:T(128)S(1)}, f32[128]{0:T(128)}, u32[]{:S(2)}) copy-start(f32[128]{0:T(128)} %param.11) | copy-start | bytes 1540
  4.5 0.7 %copy-start.5 = (s32[32]{0:T(128)S(1)}, s32[32]{0:T(128)}, u32[]{:S(2)}) copy-start(s32[32]{0:T(128)} %frames_ref.1) | copy-start | bytes 388

commit v2 on v1

v2 whole, which is shorter than its diff:
```python
import functools
import math

import jax
import jax.numpy as jnp
from jax import lax
from jax.experimental import pallas as pl
from jax.experimental.pallas import tpu as pltpu
from jax.sharding import PartitionSpec as P

HD = 128
FRAMES = 32
Z = 8
NEG = -1e30
SCALE = math.log2(math.e) / math.sqrt(HD)
EPS = 1e-05
ROW_TILE = 256
DEPTH = 1024
MESH = pl.DeviceIdType.MESH
f32 = jnp.float32
bf16 = jnp.bfloat16


def nt_dot(a, b):
    return lax.dot_general(a, b, (((1,), (1,)), ((), ())), preferred_element_type=f32)


def kernel(
    x_hbm, kw_hbm, vw_hbm, gain_hbm, q_hbm, frames_hbm, first_hbm, count_hbm,
    out_ref,
    gain_ref, frames_ref, first_ref, count_ref, xb, wb, kv, kvs, qb, feat, ka, va, m_ref, acc_ref, o_send, o_recv, l_send, l_recv,
    in_sem, q_sem, r_send, r_recv, s_send, s_recv, qx_sem, ox_sem,
):
    steps = xb.shape[1]
    rows = qb.shape[1]
    part = kv.shape[2]
    sec = lax.axis_index("section")
    blk = lax.axis_index("blk")
    head = lax.axis_index("head")
    y_hi = blk // Z
    z = lax.rem(blk, Z)
    partner_blk = (1 - y_hi) * Z + z
    right = (sec, y_hi * Z + lax.rem(z + 1, Z), head)
    left = (sec, y_hi * Z + lax.rem(z + Z - 1, Z), head)
    partner = (sec, partner_blk, head)
    sibling = (1 - sec, blk, head)

    def weight_copies(i):
        at = pl.ds(i * DEPTH, DEPTH)
        return (
            pltpu.make_async_copy(kw_hbm.at[at, :], wb.at[i, :, pl.ds(0, HD)], in_sem.at[0, i]),
            pltpu.make_async_copy(vw_hbm.at[at, :], wb.at[i, :, pl.ds(HD, HD)], in_sem.at[1, i]),
        )

    def row_copy(c, i):
        at = pl.ds(i * DEPTH, DEPTH)
        return pltpu.make_async_copy(
            x_hbm.at[pl.ds(2 * c * part, 2 * part), at], xb.at[c, i], in_sem.at[2 + c, i]
        )

    barrier = pltpu.get_barrier_semaphore()
    for other in (right, left, partner, sibling):
        pl.semaphore_signal(barrier, inc=1, device_id=other, device_id_type=MESH)

    for i in range(steps):
        for copy in weight_copies(i):
            copy.start()
        row_copy(0, i).start()
    own_q = pltpu.make_async_copy(q_hbm, qb.at[1], q_sem.at[0])
    own_q.start()
    small = [
        pltpu.make_async_copy(source, target, q_sem.at[1 + i])
        for i, (source, target) in enumerate(
            (
                (frames_hbm, frames_ref),
                (first_hbm, first_ref),
                (count_hbm, count_ref),
                (gain_hbm, gain_ref),
            )
        )
    ]
    for copy in small:
        copy.start()
    for i in range(steps):
        row_copy(1, i).start()

    def ring_copy(direction, k, source):
        return pltpu.make_async_remote_copy(
            src_ref=source, dst_ref=kv.at[1 + k // 2, 2 * (k % 2) + direction],
            send_sem=r_send.at[direction, k], recv_sem=r_recv.at[direction, k],
            device_id=(right, left)[direction], device_id_type=MESH,
        )

    def to_sibling(s):
        return pltpu.make_async_remote_copy(
            src_ref=kv.at[s], dst_ref=kvs.at[s], send_sem=s_send.at[s], recv_sem=s_recv.at[s],
            device_id=sibling, device_id_type=MESH,
        )

    q_copy = pltpu.make_async_remote_copy(
        src_ref=qb.at[1], dst_ref=qb.at[0], send_sem=qx_sem.at[0], recv_sem=qx_sem.at[1],
        device_id=partner, device_id_type=MESH,
    )
    for c in range(2):
        total = None
        for i in range(steps):
            if c == 0:
                for copy in weight_copies(i):
                    copy.wait()
            row_copy(c, i).wait()
            term = jnp.dot(xb[c, i], wb[i], preferred_element_type=f32)
            total = term if total is None else total + term
        if c == 0:
            for copy in small:
                copy.wait()
        key_raw = total[:, :HD]
        mean_square = jnp.mean(key_raw * key_raw, axis=1, keepdims=True)
        keys = (key_raw / jnp.sqrt(mean_square + EPS) * gain_ref[...]).astype(bf16)
        values = total[:, HD:].astype(bf16)
        for j in range(2):
            kv[0, 2 * c + j, :, :HD] = keys[j * part : (j + 1) * part]
            kv[0, 2 * c + j, :, HD:] = values[j * part : (j + 1) * part]
        if c == 0:
            pl.semaphore_wait(barrier, 4)
        ring_copy(0, c, kv.at[0, 2 * c]).start()
        ring_copy(1, c, kv.at[0, 2 * c + 1]).start()
        if c == 0:
            own_q.wait()
            q_copy.start()
    for c in range(2):
        ring_copy(0, 2 + c, kv.at[0, 2 * c + 1]).start()
        ring_copy(1, 2 + c, kv.at[0, 2 * c]).start()
    to_sibling(0).start()

    lane = lax.broadcasted_iota(jnp.int32, (1, HD), 1)
    starts = jnp.zeros((1, HD), jnp.int32)
    ends = jnp.zeros((1, HD), jnp.int32)
    for f in range(FRAMES):
        tokens = frames_ref[f]
        starts = starts + jnp.where(lane > f, tokens, 0)
        ends = ends + jnp.where(lane >= f, tokens, 0)
    ends = jnp.where(lane < FRAMES, ends, 0)
    heads_per_row = rows // first_ref.shape[1]
    text = first_ref.shape[1]
    spread = (
        lax.broadcasted_iota(jnp.int32, (rows, text), 0) // heads_per_row
        == lax.broadcasted_iota(jnp.int32, (rows, text), 1)
    ).astype(bf16)
    frame_id = lax.broadcasted_iota(jnp.int32, (HD, text), 0)
    for i, b in ((0, partner_blk), (1, blk)):
        first = first_ref[pl.ds(b, 1), :]
        end = jnp.minimum(first + count_ref[pl.ds(b, 1), :], FRAMES)
        closed = jnp.where((frame_id >= first) & (frame_id < end), 0.0, NEG).astype(bf16)
        feat[i] = nt_dot(spread, closed).astype(bf16)

    m_ref[...] = jnp.full_like(m_ref, 2 * NEG)
    acc_ref[...] = jnp.zeros_like(acc_ref)
    va[:, HD:] = jnp.ones_like(va[:, HD:])

    def token_base(s, sub, direction, section):
        hop = (s + 1) // 2
        odd = lax.rem(s + 1, 2)
        if direction == 0:
            source, quarter = lax.rem(z + Z - hop, Z), odd + 2 * sub
        else:
            source, quarter = lax.rem(z + hop, Z), 1 - odd + 2 * sub
        return (((section * 2 + y_hi) * Z + source) * 4 + quarter) * part

    def own_base(quarter, section):
        return (((section * 2 + y_hi) * Z + z) * 4 + quarter) * part

    def stage(slot, chunk, base):
        at = pl.ds(slot * part, part)
        pos = base + lax.broadcasted_iota(jnp.int32, (part, HD), 0)
        ka[at, :HD] = chunk[:, :HD]
        ka[at, HD:] = ((pos >= starts) & (pos < ends)).astype(bf16)
        va[at, :HD] = chunk[:, HD:]

    def attend(i, r, slot, count):
        at = pl.ds(r * ROW_TILE, ROW_TILE)
        q = jnp.concatenate([qb[i, at, :], feat[i, at, :]], axis=1)
        keys_at = pl.ds(slot * part, count * part)
        k_all = ka[keys_at, :]
        v_all = va[keys_at, :]
        s = nt_dot(q, k_all)
        m_old = m_ref[i, at, :]
        m_new = jnp.maximum(m_old, jnp.max(s, axis=1, keepdims=True))
        p = jnp.exp2((s - m_new[:, :1]) * SCALE).astype(bf16)
        fade = jnp.exp2((m_old - m_new) * SCALE)
        m_ref[i, at, :] = m_new
        pv = jnp.dot(p, v_all, preferred_element_type=f32)
        acc_ref[i, at, :] = acc_ref[i, at, :] * jnp.concatenate([fade, fade], axis=1) + pv

    tiles = rows // ROW_TILE
    for j in range(4):
        stage(j, kv[0, j], own_base(j, sec))
    for r in range(tiles):
        attend(1, r, 0, 4)
    q_copy.wait()
    for r in range(tiles):
        attend(0, r, 0, 4)

    def arrivals(s, forward):
        for sub in range(2):
            for direction in range(2):
                source = kv.at[s, 2 * sub + direction]
                ring_copy(direction, 2 * s - 2 + sub, source).wait_recv()
                if forward:
                    ring_copy(direction, 2 * s + 2 + sub, source).start()
        to_sibling(s).start()
        to_sibling(s - 1).wait_recv()

    def stage_kv(slot, s):
        for sub in range(2):
            for direction in range(2):
                j = 2 * sub + direction
                stage(slot + j, kv[s, j], token_base(s, sub, direction, sec))

    def stage_kvs(slot, s):
        for sub in range(2):
            for direction in range(2):
                j = 2 * sub + direction
                stage(slot + j, kvs[s, j], token_base(s, sub, direction, 1 - sec))

    def attend_all():
        for i in range(2):
            for r in range(tiles):
                attend(i, r, 0, 8)

    arrivals(1, True)
    stage_kv(0, 1)
    for j in range(4):
        stage(4 + j, kvs[0, j], own_base(j, 1 - sec))
    attend_all()

    def forwarding(s, carry):
        arrivals(s, True)
        stage_kv(0, s)
        stage_kvs(4, s - 1)
        attend_all()
        return carry

    lax.fori_loop(2, 6, forwarding, 0)
    arrivals(6, False)
    stage_kv(0, 6)
    stage_kvs(4, 5)
    attend_all()

    arrivals(7, False)
    stage_kv(0, 7)
    stage_kvs(4, 6)
    for r in range(tiles):
        attend(0, r, 0, 8)
    to_sibling(7).wait_recv()
    stage_kvs(8, 7)

    def o_copies(r):
        at = pl.ds(r * ROW_TILE, ROW_TILE)
        return (
            pltpu.make_async_remote_copy(
                src_ref=o_send.at[at, :], dst_ref=o_recv.at[at, :],
                send_sem=ox_sem.at[0, r], recv_sem=ox_sem.at[1, r],
                device_id=partner, device_id_type=MESH,
            ),
            pltpu.make_async_remote_copy(
                src_ref=l_send.at[r], dst_ref=l_recv.at[r],
                send_sem=ox_sem.at[2, r], recv_sem=ox_sem.at[3, r],
                device_id=partner, device_id_type=MESH,
            ),
        )

    def level(i, at):
        return m_ref[i, at, :] * SCALE + jnp.log2(acc_ref[i, at, HD:])

    for r in range(tiles):
        at = pl.ds(r * ROW_TILE, ROW_TILE)
        attend(0, r, 8, 4)
        o_send[at, :] = (acc_ref[0, at, :HD] / acc_ref[0, at, HD:]).astype(bf16)
        weight = level(0, at)
        for h in range(ROW_TILE // HD):
            l_send[r, pl.ds(8 * h, 8), :] = weight[h * HD : (h + 1) * HD].T[:8]
        for copy in o_copies(r):
            copy.start()
    for r in range(tiles):
        attend(1, r, 0, 12)
    for r in range(tiles):
        at = pl.ds(r * ROW_TILE, ROW_TILE)
        for copy in o_copies(r):
            copy.wait_recv()
        mine = level(1, at)
        theirs = jnp.concatenate(
            [
                jnp.broadcast_to(l_recv[r, 8 * h : 8 * h + 1, :], (HD, HD)).T
                for h in range(ROW_TILE // HD)
            ],
            axis=0,
        )
        top = jnp.maximum(mine, theirs)
        mine = jnp.exp2(mine - top)
        theirs = jnp.exp2(theirs - top)
        own = acc_ref[1, at, :HD] / acc_ref[1, at, HD:]
        total = (mine * own + theirs * o_recv[at, :].astype(f32)) / (mine + theirs)
        out_ref[at, :] = total.astype(bf16)

    for k in range(14):
        for direction in range(2):
            ring_copy(direction, k, kv.at[0, 0]).wait_send()
    for e in range(8):
        to_sibling(e).wait_send()
    for r in range(tiles):
        for copy in o_copies(r):
            copy.wait_send()


def body(
    projected, key_weight, value_weight, key_gain, queries, frame_tokens, span_first, span_count
):
    count, width = projected.shape
    text, sub_heads, _ = queries.shape
    rows = text * sub_heads
    part = count // 4
    steps = width // DEPTH
    out = pl.pallas_call(
        kernel,
        out_shape=jax.ShapeDtypeStruct((rows, HD), bf16),
        in_specs=[pl.BlockSpec(memory_space=pltpu.HBM)] * 8,
        out_specs=pl.BlockSpec(memory_space=pltpu.VMEM),
        scratch_shapes=[
            pltpu.VMEM((1, HD), f32),
            pltpu.SMEM((FRAMES,), jnp.int32),
            pltpu.VMEM((span_first.shape[0] // text, text), jnp.int32),
            pltpu.VMEM((span_first.shape[0] // text, text), jnp.int32),
            pltpu.VMEM((2, steps, 2 * part, DEPTH), bf16),
            pltpu.VMEM((steps, DEPTH, 2 * HD), bf16),
            pltpu.VMEM((8, 4, part, 2 * HD), bf16),
            pltpu.VMEM((8, 4, part, 2 * HD), bf16),
            pltpu.VMEM((2, rows, HD), bf16),
            pltpu.VMEM((2, rows, HD), bf16),
            pltpu.VMEM((12 * part, 2 * HD), bf16),
            pltpu.VMEM((12 * part, 2 * HD), bf16),
            pltpu.VMEM((2, rows, HD), f32),
            pltpu.VMEM((2, rows, 2 * HD), f32),
            pltpu.VMEM((rows, HD), bf16),
            pltpu.VMEM((rows, HD), bf16),
            pltpu.VMEM((rows // ROW_TILE, 8 * (ROW_TILE // HD), HD), f32),
            pltpu.VMEM((rows // ROW_TILE, 8 * (ROW_TILE // HD), HD), f32),
            pltpu.SemaphoreType.DMA((4, steps)),
            pltpu.SemaphoreType.DMA((5,)),
            pltpu.SemaphoreType.DMA((2, 14)),
            pltpu.SemaphoreType.DMA((2, 14)),
            pltpu.SemaphoreType.DMA((8,)),
            pltpu.SemaphoreType.DMA((8,)),
            pltpu.SemaphoreType.DMA((2,)),
            pltpu.SemaphoreType.DMA((4, rows // ROW_TILE)),
        ],
        compiler_params=pltpu.CompilerParams(
            collective_id=0, has_side_effects=True, vmem_limit_bytes=60 * 2**20
        ),
        name="gather_attend",
    )(
        projected, key_weight, value_weight, key_gain.reshape(1, HD),
        queries.reshape(rows, HD), frame_tokens,
        span_first.reshape(-1, text), span_count.reshape(-1, text),
    )
    return out.reshape(text, sub_heads, HD)


def solution(mesh):
    placed = (
        P(("section", "blk"), None),
        P(None, "head"),
        P(None, "head"),
        P(),
        P("blk", "section", "head"),
        P(),
        P(),
        P(),
    )
    return jax.shard_map(
        body, mesh=mesh, in_specs=placed, out_specs=P("blk", "section", "head"), check_vma=False
    )
```

time: 48.7 us -> 45.7 us (0.938)
  local copies, waits for them, and re-layouts: 5.85 us -> 1.61 us
  Pallas kernels: 42.5 us -> 44 us
    unnamed x13 -> x1, local copies, waits for them, and re-layouts: 5.85 us -> 1.61 us
    pallas_call x1, Pallas kernels: 42.5 us -> 44 us  [body(): pl.pallas_call(kernel, out_shape=jax.ShapeDtypeStruct((rows, HD), bf16),...]
where the time goes in v2:
time: 45.7 us; the launch traced here: 45.6 us
  Pallas kernels  44 us (96%)
  local copies, waits for them, and re-layouts  1.61 us (4%)
    pallas_call x1, Pallas kernels, body(): pl.pallas_call(kernel, out_shape=jax.ShapeDtypeStruct((rows, HD), bf16),...  44 us
    unnamed x1, local copies, waits for them, and re-layouts  1.61 us

profile of v2, /device:TPU:1, one launch (start us, length us, event | category | flops | bytes accessed | tf_op | source)
XLA Modules:
  0.0 45.6 jit_solution(8562690228851725367)
XLA Ops:
  0.0 44.0 %gather_attend.1 = bf16[512,128]{1,0:T(8,128)(2,1)} custom-call(bf16[512,8192]{1,0:T(8,128)(2,1)} %x_hbm.1, bf16[8192,128]{1,0:T(8,128)(2,1)} %kw_hbm.1, bf16[8192,128]{1,0:T(8,128)(2,1)} %vw_hbm.1, f32[1,128]{1,0:T(1,128)} %bitcast.9, bf16[512,128]{1,0:T(8,128)(2,1)} %bitcast.6, s32[32]{0:T(128)} %frames_hbm.1, s32[16,128]{1,0:T(8,128)} %bitcast.7, ...), custom_call_target="tpu_custom_call" | custom-call | tf_op jit(solution)/shard_map/gather_attend/pallas_call | solution.py:323
  44.0 1.6 %copy.10 = bf16[128,4,128]{2,1,0:T(4,128)(2,1)} copy(bf16[128,4,128]{2,1,0:T(4,128)(2,1)} %bitcast.5) | data formatting | bytes 262144

commit v3 on v2

--- a/solution.py
+++ b/solution.py
@@ -15,7 +15,7 @@
 SCALE = math.log2(math.e) / math.sqrt(HD)
 EPS = 1e-05
 ROW_TILE = 256
-DEPTH = 1024
+DEPTH = 2048
 MESH = pl.DeviceIdType.MESH
 f32 = jnp.float32
 bf16 = jnp.bfloat16
@@ -28,7 +28,7 @@
 def kernel(
     x_hbm, kw_hbm, vw_hbm, gain_hbm, q_hbm, frames_hbm, first_hbm, count_hbm,
     out_ref,
-    gain_ref, frames_ref, first_ref, count_ref, xb, wb, kv, kvs, qb, feat, ka, va, m_ref, acc_ref, o_send, o_recv, l_send, l_recv,
+    gain_ref, frames_ref, first_ref, count_ref, xb, wb, raw, kv, kvs, qb, feat, ka, va, m_ref, acc_ref, o_send, o_recv, l_send, l_recv,
     in_sem, q_sem, r_send, r_recv, s_send, s_recv, qx_sem, ox_sem,
 ):
     steps = xb.shape[1]
@@ -53,19 +53,26 @@
         )
 
     def row_copy(c, i):
-        at = pl.ds(i * DEPTH, DEPTH)
+        at = pl.ds(pl.multiple_of(2 * c * part, part), 2 * part)
         return pltpu.make_async_copy(
-            x_hbm.at[pl.ds(2 * c * part, 2 * part), at], xb.at[c, i], in_sem.at[2 + c, i]
+            x_hbm.at[at, pl.ds(i * DEPTH, DEPTH)], xb.at[c, i], in_sem.at[2 + c, i]
         )
 
     barrier = pltpu.get_barrier_semaphore()
     for other in (right, left, partner, sibling):
         pl.semaphore_signal(barrier, inc=1, device_id=other, device_id_type=MESH)
 
-    for i in range(steps):
+    def start_inputs(i, carry):
         for copy in weight_copies(i):
             copy.start()
         row_copy(0, i).start()
+        return carry
+
+    def start_rest(i, carry):
+        row_copy(1, i).start()
+        return carry
+
+    lax.fori_loop(0, steps, start_inputs, 0)
     own_q = pltpu.make_async_copy(q_hbm, qb.at[1], q_sem.at[0])
     own_q.start()
     small = [
@@ -81,8 +88,7 @@
     ]
     for copy in small:
         copy.start()
-    for i in range(steps):
-        row_copy(1, i).start()
+    lax.fori_loop(0, steps, start_rest, 0)
 
     def ring_copy(direction, k, source):
         return pltpu.make_async_remote_copy(
@@ -101,32 +107,41 @@
         src_ref=qb.at[1], dst_ref=qb.at[0], send_sem=qx_sem.at[0], recv_sem=qx_sem.at[1],
         device_id=partner, device_id_type=MESH,
     )
-    for c in range(2):
-        total = None
-        for i in range(steps):
-            if c == 0:
+    raw[...] = jnp.zeros_like(raw)
+
+    def half(c, carry):
+        def project(i, carry):
+            @pl.when(c == 0)
+            def _():
                 for copy in weight_copies(i):
                     copy.wait()
+
             row_copy(c, i).wait()
-            term = jnp.dot(xb[c, i], wb[i], preferred_element_type=f32)
-            total = term if total is None else total + term
-        if c == 0:
-            for copy in small:
-                copy.wait()
-        key_raw = total[:, :HD]
-        mean_square = jnp.mean(key_raw * key_raw, axis=1, keepdims=True)
-        keys = (key_raw / jnp.sqrt(mean_square + EPS) * gain_ref[...]).astype(bf16)
-        values = total[:, HD:].astype(bf16)
+
+            @pl.when((c == 0) & (i == steps - 1))
+            def _():
+                pl.semaphore_wait(barrier, 4)
+                own_q.wait()
+                q_copy.start()
+                for copy in small:
+                    copy.wait()
+
+            at = pl.ds(pl.multiple_of(2 * c * part, part), 2 * part)
+            raw[at, :] += jnp.dot(xb[c, i], wb[i], preferred_element_type=f32)
+            return carry
+
+        lax.fori_loop(0, steps, project, 0)
         for j in range(2):
-            kv[0, 2 * c + j, :, :HD] = keys[j * part : (j + 1) * part]
-            kv[0, 2 * c + j, :, HD:] = values[j * part : (j + 1) * part]
-        if c == 0:
-            pl.semaphore_wait(barrier, 4)
-        ring_copy(0, c, kv.at[0, 2 * c]).start()
-        ring_copy(1, c, kv.at[0, 2 * c + 1]).start()
-        if c == 0:
-            own_q.wait()
-            q_copy.start()
+            at = pl.ds(pl.multiple_of((2 * c + j) * part, part), part)
+            key_raw = raw[at, :HD]
+            mean_square = jnp.mean(key_raw * key_raw, axis=1, keepdims=True)
+            keys = key_raw / jnp.sqrt(mean_square + EPS) * gain_ref[...]
+            kv[0, 2 * c + j, :, :HD] = keys.astype(bf16)
+            kv[0, 2 * c + j, :, HD:] = raw[at, HD:].astype(bf16)
+            ring_copy(j, c, kv.at[0, 2 * c + j]).start()
+        return carry
+
+    lax.fori_loop(0, 2, half, 0)
     for c in range(2):
         ring_copy(0, 2 + c, kv.at[0, 2 * c + 1]).start()
         ring_copy(1, 2 + c, kv.at[0, 2 * c]).start()
@@ -206,7 +221,11 @@
                 source = kv.at[s, 2 * sub + direction]
                 ring_copy(direction, 2 * s - 2 + sub, source).wait_recv()
                 if forward:
-                    ring_copy(direction, 2 * s + 2 + sub, source).start()
+
+                    @pl.when(s <= 5)
+                    def _():
+                        ring_copy(direction, 2 * s + 2 + sub, source).start()
+
         to_sibling(s).start()
         to_sibling(s - 1).wait_recv()
 
@@ -240,11 +259,7 @@
         attend_all()
         return carry
 
-    lax.fori_loop(2, 6, forwarding, 0)
-    arrivals(6, False)
-    stage_kv(0, 6)
-    stage_kvs(4, 5)
-    attend_all()
+    lax.fori_loop(2, 7, forwarding, 0)
 
     arrivals(7, False)
     stage_kv(0, 7)
@@ -332,6 +347,7 @@
             pltpu.VMEM((span_first.shape[0] // text, text), jnp.int32),
             pltpu.VMEM((2, steps, 2 * part, DEPTH), bf16),
             pltpu.VMEM((steps, DEPTH, 2 * HD), bf16),
+            pltpu.VMEM((count, 2 * HD), f32),
             pltpu.VMEM((8, 4, part, 2 * HD), bf16),
             pltpu.VMEM((8, 4, part, 2 * HD), bf16),
             pltpu.VMEM((2, rows, HD), bf16),

time: 45.7 us -> 44.5 us (0.974)
  Pallas kernels: 44 us -> 42.8 us
    pallas_call x1, Pallas kernels: 44 us -> 42.8 us  [body(): pl.pallas_call(kernel, out_shape=jax.ShapeDtypeStruct((rows, HD), bf16),...]
where the time goes in v3:
time: 44.5 us
  Pallas kernels  42.8 us (96%)
  local copies, waits for them, and re-layouts  1.61 us (4%)
    pallas_call x1, Pallas kernels, body(): pl.pallas_call(kernel, out_shape=jax.ShapeDtypeStruct((rows, HD), bf16),...  42.8 us
    unnamed x1, local copies, waits for them, and re-layouts  1.61 us

profile of v3, /device:TPU:1, one launch (start us, length us, event | category | flops | bytes accessed | tf_op | source)
XLA Modules:
  0.0 44.5 jit_solution(15999258437255800784)
XLA Ops:
  0.0 42.8 %gather_attend.1 = bf16[512,128]{1,0:T(8,128)(2,1)} custom-call(bf16[512,8192]{1,0:T(8,128)(2,1)} %x_hbm.1, bf16[8192,128]{1,0:T(8,128)(2,1)} %kw_hbm.1, bf16[8192,128]{1,0:T(8,128)(2,1)} %vw_hbm.1, f32[1,128]{1,0:T(1,128)} %bitcast.9, bf16[512,128]{1,0:T(8,128)(2,1)} %bitcast.6, s32[32]{0:T(128)} %frames_hbm.1, s32[16,128]{1,0:T(8,128)} %bitcast.7, ...), custom_call_target="tpu_custom_call" | custom-call | tf_op jit(solution)/shard_map/gather_attend/pallas_call | solution.py:338
  42.9 1.6 %copy.10 = bf16[128,4,128]{2,1,0:T(4,128)(2,1)} copy(bf16[128,4,128]{2,1,0:T(4,128)(2,1)} %bitcast.5) | data formatting | bytes 262144

commit v4 on v3

--- a/solution.py
+++ b/solution.py
@@ -72,7 +72,6 @@
         row_copy(1, i).start()
         return carry
 
-    lax.fori_loop(0, steps, start_inputs, 0)
     own_q = pltpu.make_async_copy(q_hbm, qb.at[1], q_sem.at[0])
     own_q.start()
     small = [
@@ -88,6 +87,7 @@
     ]
     for copy in small:
         copy.start()
+    lax.fori_loop(0, steps, start_inputs, 0)
     lax.fori_loop(0, steps, start_rest, 0)
 
     def ring_copy(direction, k, source):
@@ -107,6 +107,14 @@
         src_ref=qb.at[1], dst_ref=qb.at[0], send_sem=qx_sem.at[0], recv_sem=qx_sem.at[1],
         device_id=partner, device_id_type=MESH,
     )
+    def last_to_sibling(sub):
+        at = pl.ds(2 * sub, 2)
+        return pltpu.make_async_remote_copy(
+            src_ref=kv.at[7, at], dst_ref=kvs.at[7, at],
+            send_sem=s_send.at[7 + sub], recv_sem=s_recv.at[7 + sub],
+            device_id=sibling, device_id_type=MESH,
+        )
+
     raw[...] = jnp.zeros_like(raw)
 
     def half(c, carry):
@@ -261,12 +269,17 @@
 
     lax.fori_loop(2, 7, forwarding, 0)
 
-    arrivals(7, False)
+    for sub in range(2):
+        for direction in range(2):
+            ring_copy(direction, 12 + sub, kv.at[7, 2 * sub + direction]).wait_recv()
+        last_to_sibling(sub).start()
+    to_sibling(6).wait_recv()
     stage_kv(0, 7)
     stage_kvs(4, 6)
     for r in range(tiles):
         attend(0, r, 0, 8)
-    to_sibling(7).wait_recv()
+    for sub in range(2):
+        last_to_sibling(sub).wait_recv()
     stage_kvs(8, 7)
 
     def o_copies(r):
@@ -320,8 +333,10 @@
     for k in range(14):
         for direction in range(2):
             ring_copy(direction, k, kv.at[0, 0]).wait_send()
-    for e in range(8):
+    for e in range(7):
         to_sibling(e).wait_send()
+    for sub in range(2):
+        last_to_sibling(sub).wait_send()
     for r in range(tiles):
         for copy in o_copies(r):
             copy.wait_send()
@@ -364,8 +379,8 @@
             pltpu.SemaphoreType.DMA((5,)),
             pltpu.SemaphoreType.DMA((2, 14)),
             pltpu.SemaphoreType.DMA((2, 14)),
-            pltpu.SemaphoreType.DMA((8,)),
-            pltpu.SemaphoreType.DMA((8,)),
+            pltpu.SemaphoreType.DMA((9,)),
+            pltpu.SemaphoreType.DMA((9,)),
             pltpu.SemaphoreType.DMA((2,)),
             pltpu.SemaphoreType.DMA((4, rows // ROW_TILE)),
         ],

time: 44.5 us -> 44.6 us (level)
  no operation moved by 1% of the time
where the time goes in v4:
time: 44.6 us
  Pallas kernels  42.9 us (96%)
  local copies, waits for them, and re-layouts  1.61 us (4%)
    pallas_call x1, Pallas kernels, body(): pl.pallas_call(kernel, out_shape=jax.ShapeDtypeStruct((rows, HD), bf16),...  42.9 us
    unnamed x1, local copies, waits for them, and re-layouts  1.61 us

profile of v4, /device:TPU:1, one launch (start us, length us, event | category | flops | bytes accessed | tf_op | source)
XLA Modules:
  0.0 44.6 jit_solution(4039804269746427264)
XLA Ops:
  0.0 42.9 %gather_attend.1 = bf16[512,128]{1,0:T(8,128)(2,1)} custom-call(bf16[512,8192]{1,0:T(8,128)(2,1)} %x_hbm.1, bf16[8192,128]{1,0:T(8,128)(2,1)} %kw_hbm.1, bf16[8192,128]{1,0:T(8,128)(2,1)} %vw_hbm.1, f32[1,128]{1,0:T(1,128)} %bitcast.9, bf16[512,128]{1,0:T(8,128)(2,1)} %bitcast.6, s32[32]{0:T(128)} %frames_hbm.1, s32[16,128]{1,0:T(8,128)} %bitcast.7, ...), custom_call_target="tpu_custom_call" | custom-call | tf_op jit(solution)/shard_map/gather_attend/pallas_call | solution.py:353
  42.9 1.6 %copy.10 = bf16[128,4,128]{2,1,0:T(4,128)(2,1)} copy(bf16[128,4,128]{2,1,0:T(4,128)(2,1)} %bitcast.5) | data formatting | bytes 262144

commit v5 on v3

--- a/solution.py
+++ b/solution.py
@@ -72,7 +72,6 @@
         row_copy(1, i).start()
         return carry
 
-    lax.fori_loop(0, steps, start_inputs, 0)
     own_q = pltpu.make_async_copy(q_hbm, qb.at[1], q_sem.at[0])
     own_q.start()
     small = [
@@ -88,6 +87,7 @@
     ]
     for copy in small:
         copy.start()
+    lax.fori_loop(0, steps, start_inputs, 0)
     lax.fori_loop(0, steps, start_rest, 0)
 
     def ring_copy(direction, k, source):
@@ -136,15 +136,16 @@
             key_raw = raw[at, :HD]
             mean_square = jnp.mean(key_raw * key_raw, axis=1, keepdims=True)
             keys = key_raw / jnp.sqrt(mean_square + EPS) * gain_ref[...]
-            kv[0, 2 * c + j, :, :HD] = keys.astype(bf16)
-            kv[0, 2 * c + j, :, HD:] = raw[at, HD:].astype(bf16)
-            ring_copy(j, c, kv.at[0, 2 * c + j]).start()
+            slot = 2 * c + 1 - j
+            kv[0, slot, :, :HD] = keys.astype(bf16)
+            kv[0, slot, :, HD:] = raw[at, HD:].astype(bf16)
+            ring_copy(j, c, kv.at[0, slot]).start()
         return carry
 
     lax.fori_loop(0, 2, half, 0)
     for c in range(2):
-        ring_copy(0, 2 + c, kv.at[0, 2 * c + 1]).start()
-        ring_copy(1, 2 + c, kv.at[0, 2 * c]).start()
+        ring_copy(0, 2 + c, kv.at[0, 2 * c]).start()
+        ring_copy(1, 2 + c, kv.at[0, 2 * c + 1]).start()
     to_sibling(0).start()
 
     lane = lax.broadcasted_iota(jnp.int32, (1, HD), 1)
@@ -181,9 +182,6 @@
             source, quarter = lax.rem(z + hop, Z), 1 - odd + 2 * sub
         return (((section * 2 + y_hi) * Z + source) * 4 + quarter) * part
 
-    def own_base(quarter, section):
-        return (((section * 2 + y_hi) * Z + z) * 4 + quarter) * part
-
     def stage(slot, chunk, base):
         at = pl.ds(slot * part, part)
         pos = base + lax.broadcasted_iota(jnp.int32, (part, HD), 0)
@@ -207,24 +205,15 @@
         acc_ref[i, at, :] = acc_ref[i, at, :] * jnp.concatenate([fade, fade], axis=1) + pv
 
     tiles = rows // ROW_TILE
-    for j in range(4):
-        stage(j, kv[0, j], own_base(j, sec))
-    for r in range(tiles):
-        attend(1, r, 0, 4)
-    q_copy.wait()
-    for r in range(tiles):
-        attend(0, r, 0, 4)
-
-    def arrivals(s, forward):
+    def arrivals(s):
         for sub in range(2):
             for direction in range(2):
                 source = kv.at[s, 2 * sub + direction]
                 ring_copy(direction, 2 * s - 2 + sub, source).wait_recv()
-                if forward:
-
-                    @pl.when(s <= 5)
-                    def _():
-                        ring_copy(direction, 2 * s + 2 + sub, source).start()
+
+                @pl.when(s <= 5)
+                def _():
+                    ring_copy(direction, 2 * s + 2 + sub, source).start()
 
         to_sibling(s).start()
         to_sibling(s - 1).wait_recv()
@@ -246,22 +235,23 @@
             for r in range(tiles):
                 attend(i, r, 0, 8)
 
-    arrivals(1, True)
-    stage_kv(0, 1)
-    for j in range(4):
-        stage(4 + j, kvs[0, j], own_base(j, 1 - sec))
-    attend_all()
-
-    def forwarding(s, carry):
-        arrivals(s, True)
+    stage_kv(0, 0)
+    for r in range(tiles):
+        attend(1, r, 0, 4)
+    arrivals(1)
+    q_copy.wait()
+    for r in range(tiles):
+        attend(0, r, 0, 4)
+
+    def turn(s, carry):
         stage_kv(0, s)
         stage_kvs(4, s - 1)
         attend_all()
+        arrivals(s + 1)
         return carry
 
-    lax.fori_loop(2, 7, forwarding, 0)
-
-    arrivals(7, False)
+    lax.fori_loop(1, 7, turn, 0)
+
     stage_kv(0, 7)
     stage_kvs(4, 6)
     for r in range(tiles):

time: 44.5 us -> 44.7 us (level)
  no operation moved by 1% of the time
where the time goes in v5:
time: 44.7 us; the launch traced here: 44.6 us
  Pallas kernels  43 us (96%)
  local copies, waits for them, and re-layouts  1.61 us (4%)
    pallas_call x1, Pallas kernels, body(): pl.pallas_call(kernel, out_shape=jax.ShapeDtypeStruct((rows, HD), bf16),...  43 us
    unnamed x1, local copies, waits for them, and re-layouts  1.61 us

profile of v5, /device:TPU:1, one launch (start us, length us, event | category | flops | bytes accessed | tf_op | source)
XLA Modules:
  0.0 44.6 jit_solution(2662537281402226063)
XLA Ops:
  0.0 43.0 %gather_attend.1 = bf16[512,128]{1,0:T(8,128)(2,1)} custom-call(bf16[512,8192]{1,0:T(8,128)(2,1)} %x_hbm.1, bf16[8192,128]{1,0:T(8,128)(2,1)} %kw_hbm.1, bf16[8192,128]{1,0:T(8,128)(2,1)} %vw_hbm.1, f32[1,128]{1,0:T(1,128)} %bitcast.9, bf16[512,128]{1,0:T(8,128)(2,1)} %bitcast.6, s32[32]{0:T(128)} %frames_hbm.1, s32[16,128]{1,0:T(8,128)} %bitcast.7, ...), custom_call_target="tpu_custom_call" | custom-call | tf_op jit(solution)/shard_map/gather_attend/pallas_call | solution.py:328
  43.0 1.6 %copy.10 = bf16[128,4,128]{2,1,0:T(4,128)(2,1)} copy(bf16[128,4,128]{2,1,0:T(4,128)(2,1)} %bitcast.5) | data formatting | bytes 262144

commit v6 on v5

--- a/solution.py
+++ b/solution.py
@@ -97,9 +97,11 @@
             device_id=(right, left)[direction], device_id_type=MESH,
         )
 
-    def to_sibling(s):
+    def to_sibling(s, sub):
+        at = pl.ds(2 * sub, 2)
         return pltpu.make_async_remote_copy(
-            src_ref=kv.at[s], dst_ref=kvs.at[s], send_sem=s_send.at[s], recv_sem=s_recv.at[s],
+            src_ref=kv.at[s, at], dst_ref=kvs.at[s, at],
+            send_sem=s_send.at[s, sub], recv_sem=s_recv.at[s, sub],
             device_id=sibling, device_id_type=MESH,
         )
 
@@ -146,7 +148,8 @@
     for c in range(2):
         ring_copy(0, 2 + c, kv.at[0, 2 * c]).start()
         ring_copy(1, 2 + c, kv.at[0, 2 * c + 1]).start()
-    to_sibling(0).start()
+    for sub in range(2):
+        to_sibling(0, sub).start()
 
     lane = lax.broadcasted_iota(jnp.int32, (1, HD), 1)
     starts = jnp.zeros((1, HD), jnp.int32)
@@ -205,6 +208,7 @@
         acc_ref[i, at, :] = acc_ref[i, at, :] * jnp.concatenate([fade, fade], axis=1) + pv
 
     tiles = rows // ROW_TILE
+
     def arrivals(s):
         for sub in range(2):
             for direction in range(2):
@@ -215,8 +219,9 @@
                 def _():
                     ring_copy(direction, 2 * s + 2 + sub, source).start()
 
-        to_sibling(s).start()
-        to_sibling(s - 1).wait_recv()
+            to_sibling(s, sub).start()
+        for sub in range(2):
+            to_sibling(s - 1, sub).wait_recv()
 
     def stage_kv(slot, s):
         for sub in range(2):
@@ -256,7 +261,8 @@
     stage_kvs(4, 6)
     for r in range(tiles):
         attend(0, r, 0, 8)
-    to_sibling(7).wait_recv()
+    for sub in range(2):
+        to_sibling(7, sub).wait_recv()
     stage_kvs(8, 7)
 
     def o_copies(r):
@@ -311,7 +317,8 @@
         for direction in range(2):
             ring_copy(direction, k, kv.at[0, 0]).wait_send()
     for e in range(8):
-        to_sibling(e).wait_send()
+        for sub in range(2):
+            to_sibling(e, sub).wait_send()
     for r in range(tiles):
         for copy in o_copies(r):
             copy.wait_send()
@@ -354,8 +361,8 @@
             pltpu.SemaphoreType.DMA((5,)),
             pltpu.SemaphoreType.DMA((2, 14)),
             pltpu.SemaphoreType.DMA((2, 14)),
-            pltpu.SemaphoreType.DMA((8,)),
-            pltpu.SemaphoreType.DMA((8,)),
+            pltpu.SemaphoreType.DMA((8, 2)),
+            pltpu.SemaphoreType.DMA((8, 2)),
             pltpu.SemaphoreType.DMA((2,)),
             pltpu.SemaphoreType.DMA((4, rows // ROW_TILE)),
         ],

time: 44.7 us -> 44.8 us (level)
  no operation moved by 1% of the time
where the time goes in v6:
time: 44.8 us; the launch traced here: 44.7 us
  Pallas kernels  43.1 us (96%)
  local copies, waits for them, and re-layouts  1.61 us (4%)
    pallas_call x1, Pallas kernels, body(): pl.pallas_call(kernel, out_shape=jax.ShapeDtypeStruct((rows, HD), bf16),...  43.1 us
    unnamed x1, local copies, waits for them, and re-layouts  1.61 us

profile of v6, /device:TPU:1, one launch (start us, length us, event | category | flops | bytes accessed | tf_op | source)
XLA Modules:
  0.0 44.7 jit_solution(524242463019808468)
XLA Ops:
  0.0 43.1 %gather_attend.1 = bf16[512,128]{1,0:T(8,128)(2,1)} custom-call(bf16[512,8192]{1,0:T(8,128)(2,1)} %x_hbm.1, bf16[8192,128]{1,0:T(8,128)(2,1)} %kw_hbm.1, bf16[8192,128]{1,0:T(8,128)(2,1)} %vw_hbm.1, f32[1,128]{1,0:T(1,128)} %bitcast.9, bf16[512,128]{1,0:T(8,128)(2,1)} %bitcast.6, s32[32]{0:T(128)} %frames_hbm.1, s32[16,128]{1,0:T(8,128)} %bitcast.7, ...), custom_call_target="tpu_custom_call" | custom-call | tf_op jit(solution)/shard_map/gather_attend/pallas_call | solution.py:335
  43.1 1.6 %copy.10 = bf16[128,4,128]{2,1,0:T(4,128)(2,1)} copy(bf16[128,4,128]{2,1,0:T(4,128)(2,1)} %bitcast.5) | data formatting | bytes 262144
